TPU v7x, 32 devices: a whole 2x2x4 slice. The times are simulated.
32 devices in a mesh: groups: 2 (over y), sector: 4 (over z), term: 2 (over x), rep: 2 (over core).
Axes of the slice: x: 2, y: 2, z: 4, core: 2. Of those that a mesh axis runs over, the one named last changes fastest.
Arguments:
- start_vector: bfloat16 [8, 4, 256, 256], P(('groups', 'sector'), None, None, 'rep'), parts along dimension 0, may hold values from -3600 to 3600
- precond: bfloat16 [8, 4, 256, 256], P(('groups', 'sector'), None, None, 'rep'), parts along dimension 0, may hold values from 0.5 to 4
- left_env: bfloat16 [2, 8, 4, 256, 256], P('term', ('groups', 'sector')), parts along dimension 1, may hold values from -6 to 6, as said below
- right_env: bfloat16 [2, 4, 8, 256, 256], P('term', 'sector', 'groups', None, 'rep'), parts along dimension 2, may hold values from -6 to 6, as said below
- blocks_used: int32 [2, 8, 4], P('term', ('groups', 'sector')), parts along dimension 1, may hold values 0 or 1
Outputs:
- next_vector: float32 [8, 4, 256, 256], P(('groups', 'sector'), None, None, 'rep'), parts along dimension 0
- next_image: float32 [8, 4, 256, 256], P(('groups', 'sector'), None, None, 'rep'), parts along dimension 0
- ritz_value: float32 [2], P('groups'), parts along dimension 0
There are 2 independent parts, one for each index of `groups`. A program takes and returns all parts, laid end to end along the dimension named above; each array names one. Nothing has to cross between parts.
Inputs may be any that keep to these rules, and one draw needn't show every extreme that they name: `left_env`: each block of every term is symmetric in its two bond indices. `right_env`: each block of every term is symmetric in its two bond indices.
All inputs are finite; a program needn't handle non-finite values. No bound on the sum of `blocks_used` on one device may be relied on, other than what follows from the above.
Results may differ from a plain program's by a relative error of at most 0.0029.
The roundings to bfloat16 on the way count: a program that leaves them out, or rounds other values in their place, can miss the bound.
Values may be sent and summed in bfloat16 or wider, within the bound.
A program may use at most 64 MiB of HBM per device.

v0:
```python
import jax
import jax.numpy as jnp
from jax import lax
from jax.sharding import PartitionSpec as P

eps = 1e-06


def apply_h(vector, left_env, right_env, blocks_used):
    rounded = vector.astype(jnp.bfloat16)
    mixed = jnp.einsum("tijab,ijbc->tijac", left_env, rounded, preferred_element_type=jnp.float32)
    mixed = (mixed * blocks_used[:, :, :, None, None].astype(jnp.float32)).astype(jnp.bfloat16)
    partial_sums = jnp.einsum(
        "tijac,tjidc->ijad",
        lax.all_to_all(mixed, "sector", split_axis=2, concat_axis=1, tiled=True),
        right_env,
        preferred_element_type=jnp.float32,
    )
    halves = lax.psum_scatter(partial_sums, "rep", scatter_dimension=3, tiled=True)
    totals = lax.psum(halves, "term")
    result = lax.all_to_all(totals, "sector", split_axis=0, concat_axis=1, tiled=True)
    return result


def orthonormal(target, bases, count):
    local_terms = jnp.stack([jnp.sum(basis * target) for basis in bases])
    coefs = lax.psum(local_terms, ("sector", "rep")) / count
    rest = target
    for index, basis in enumerate(bases):
        rest = rest - coefs[index] * basis
    length = lax.psum(jnp.sum(rest * rest), ("sector", "rep")) / count
    return rest / jnp.sqrt(length + eps)


def local(start_vector, precond, left_env, right_env, blocks_used):
    count = start_vector.size * lax.axis_size("sector") * lax.axis_size("rep")
    vector = start_vector.astype(jnp.float32)
    square = lax.psum(jnp.sum(vector * vector), ("sector", "rep"))
    vzero = vector / jnp.sqrt(square / count + eps)
    scaling = precond.astype(jnp.float32)
    sigma_zero = apply_h(vzero, left_env, right_env, blocks_used)
    theta = lax.psum(jnp.sum(vzero * sigma_zero), ("sector", "rep")) / count
    vone = orthonormal((sigma_zero - theta * vzero) / scaling, (vzero,), count)
    sigma_one = apply_h(vone, left_env, right_env, blocks_used)
    cross, diag_one = lax.psum(
        (jnp.sum(vone * sigma_zero), jnp.sum(vone * sigma_one)), ("sector", "rep")
    )
    cross = cross / count
    diag_one = diag_one / count
    half_gap = (theta - diag_one) * 0.5
    lowest = (theta + diag_one) * 0.5 - jnp.sqrt(half_gap * half_gap + cross * cross)
    length = jnp.sqrt(cross * cross + (lowest - theta) * (lowest - theta))
    coef_zero = cross / length
    coef_one = (lowest - theta) / length
    residual_one = (
        coef_zero * sigma_zero
        + coef_one * sigma_one
        - lowest * (coef_zero * vzero + coef_one * vone)
    )
    vtwo = orthonormal(residual_one / scaling, (vzero, vone), count)
    sigma_two = apply_h(vtwo, left_env, right_env, blocks_used)
    return (vtwo, sigma_two, jnp.reshape(lowest, (1,)))


def solution(mesh):
    in_specs = (
        P(("groups", "sector"), None, None, "rep"),
        P(("groups", "sector"), None, None, "rep"),
        P("term", ("groups", "sector"), None, None, None),
        P("term", "sector", "groups", None, "rep"),
        P("term", ("groups", "sector"), None),
    )
    out_specs = (
        P(("groups", "sector"), None, None, "rep"),
        P(("groups", "sector"), None, None, "rep"),
        P("groups"),
    )
    return jax.shard_map(local, mesh=mesh, in_specs=in_specs, out_specs=out_specs, check_vma=False)
```

profile of v0, /device:TPU:1, one launch (start us, length us, event | category | flops | bytes accessed | tf_op | source)
XLA Modules:
  0.0 349.0 jit_solution(10617724949319841441)
XLA Ops:
  7.2 1.8 fusion.9
  9.0 15.2 %psum.77 = f32[]{:T(128)} all-reduce(f32[]{:T(128)} %fusion.9), channel_id=1, replica_groups=mesh['groups'=2,'sector'=4,'term'=2,'rep'=2] {'sector','rep'}, use_global_device_ids=true, to_apply=%region_1.0 | all-reduce | flops 1 | bytes 8 | tf_op jit(solution)/shard_map/psum | solution.py:38
  25.9 9.9 %all_to_all.63 = bf16[1,1,4,256,128]{3,4,0,1,2:T(8,128)(2,1)S(1)} all-to-all(bf16[1,1,4,256,128]{3,4,0,1,2:T(8,128)(2,1)S(1)} %fusion.6), channel_id=1, replica_groups=mesh['groups'=2,'sector'=4,'term'=2,'rep'=2] {'sector'}, dimensions={2} | all-to-all | bytes 524288 | tf_op jit(solution)/shard_map/all_to_all | solution.py:15
  35.8 1.3 convolution_bitcast_fusion.2
  37.2 11.2 %reduce-scatter.4.cloned.1.call-done = f32[4,1,256,128]{3,2,0,1:T(8,128)} async-done(((f32[4,1,256,256]{3,2,0,1:T(8,128)}), f32[4,1,256,128]{3,2,0,1:T(8,128)}) %reduce-scatter.4.cloned.1.call-update) | async-done | bytes 524304 | tf_op jit(solution)/shard_map/reduce_scatter | solution.py:19
  48.4 31.7 %all-reduce.5.cloned.1.call-done = f32[4,1,256,128]{3,2,0,1:T(8,128)} async-done(((f32[4,1,256,128]{3,2,0,1:T(8,128)}), f32[4,1,256,128]{3,2,0,1:T(8,128)}) %all-reduce.5.cloned.1.call-update) | async-done | bytes 524304 | tf_op jit(solution)/shard_map/psum | solution.py:20
  80.2 18.0 %all_to_all.64 = f32[4,1,256,128]{3,2,1,0:T(8,128)S(1)} all-to-all(f32[4,1,256,128]{3,2,1,0:T(8,128)} %bitcast.122), channel_id=1, replica_groups=mesh['groups'=2,'sector'=4,'term'=2,'rep'=2] {'sector'}, dimensions={0} | all-to-all | bytes 1048576 | tf_op jit(solution)/shard_map/all_to_all | solution.py:21
  98.9 15.4 %psum.79 = f32[]{:T(128)} all-reduce(f32[]{:T(128)} %fusion.13), channel_id=1, replica_groups=mesh['groups'=2,'sector'=4,'term'=2,'rep'=2] {'sector','rep'}, use_global_device_ids=true, to_apply=%region_5.0 | all-reduce | flops 1 | bytes 8 | tf_op jit(solution)/shard_map/psum | solution.py:42
  115.6 14.7 %psum.80 = f32[1]{0:T(128)} all-reduce(f32[1]{0:T(128)} %bitcast.11), channel_id=1, replica_groups=mesh['groups'=2,'sector'=4,'term'=2,'rep'=2] {'sector','rep'}, use_global_device_ids=true, to_apply=%region_7.0 | all-reduce | flops 1 | bytes 8 | tf_op jit(solution)/shard_map/psum | solution.py:27
  131.8 14.2 %psum.81 = f32[]{:T(128)} all-reduce(f32[]{:T(128)} %get-tuple-element.12), channel_id=1, replica_groups=mesh['groups'=2,'sector'=4,'term'=2,'rep'=2] {'sector','rep'}, use_global_device_ids=true, to_apply=%region_9.0 | all-reduce | flops 1 | bytes 8 | tf_op jit(solution)/shard_map/psum | solution.py:31
  147.0 9.4 %all_to_all.65 = bf16[1,1,4,256,128]{3,4,0,1,2:T(8,128)(2,1)S(1)} all-to-all(bf16[1,1,4,256,128]{3,4,0,1,2:T(8,128)(2,1)S(1)} %fusion.7), channel_id=1, replica_groups=mesh['groups'=2,'sector'=4,'term'=2,'rep'=2] {'sector'}, dimensions={2} | all-to-all | bytes 524288 | tf_op jit(solution)/shard_map/all_to_all | solution.py:15
  156.4 1.3 convolution_bitcast_fusion.1
  157.8 9.3 %reduce-scatter.6.cloned.1.call-done = f32[4,1,256,128]{3,2,0,1:T(8,128)} async-done(((f32[4,1,256,256]{3,2,0,1:T(8,128)}), f32[4,1,256,128]{3,2,0,1:T(8,128)}) %reduce-scatter.6.cloned.1.call-update) | async-done | bytes 524304 | tf_op jit(solution)/shard_map/reduce_scatter | solution.py:19
  167.1 31.6 %all-reduce.7.cloned.1.call-done = f32[4,1,256,128]{3,2,0,1:T(8,128)} async-done(((f32[4,1,256,128]{3,2,0,1:T(8,128)}), f32[4,1,256,128]{3,2,0,1:T(8,128)}) %all-reduce.7.cloned.1.call-update) | async-done | bytes 524304 | tf_op jit(solution)/shard_map/psum | solution.py:20
  198.7 18.0 %all_to_all.66 = f32[4,1,256,128]{3,2,1,0:T(8,128)S(1)} all-to-all(f32[4,1,256,128]{3,2,1,0:T(8,128)} %bitcast.123), channel_id=1, replica_groups=mesh['groups'=2,'sector'=4,'term'=2,'rep'=2] {'sector'}, dimensions={0} | all-to-all | bytes 1048576 | tf_op jit(solution)/shard_map/all_to_all | solution.py:21
  217.5 15.4 %all-reduce = (f32[]{:T(128)}, f32[]{:T(128)}) all-reduce(f32[]{:T(128)} %get-tuple-element.6, f32[]{:T(128)} %get-tuple-element.5), channel_id=1, replica_groups=mesh['groups'=2,'sector'=4,'term'=2,'rep'=2] {'sector','rep'}, use_global_device_ids=true, to_apply=%region_15.0 | all-reduce | flops 2 | bytes 16 | tf_op jit(solution)/shard_map/psum | solution.py:45
  236.6 1.4 pad_maximum_fusion
  238.0 14.0 %psum.85 = f32[2]{0:T(128)S(1)} all-reduce(f32[2]{0:T(128)S(1)} %pad_maximum_fusion), channel_id=1, replica_groups=mesh['groups'=2,'sector'=4,'term'=2,'rep'=2] {'sector','rep'}, use_global_device_ids=true, to_apply=%region_18.0 | all-reduce | flops 2 | bytes 16 | tf_op jit(solution)/shard_map/psum | solution.py:27
  252.6 2.1 multiply_reduce_fusion
  254.8 14.2 %psum.86 = f32[]{:T(128)} all-reduce(f32[]{:T(128)} %get-tuple-element.9), channel_id=1, replica_groups=mesh['groups'=2,'sector'=4,'term'=2,'rep'=2] {'sector','rep'}, use_global_device_ids=true, to_apply=%region_20.0 | all-reduce | flops 1 | bytes 8 | tf_op jit(solution)/shard_map/psum | solution.py:31
  270.5 9.4 %all_to_all.67 = bf16[1,1,4,256,128]{3,4,0,1,2:T(8,128)(2,1)S(1)} all-to-all(bf16[1,1,4,256,128]{3,4,0,1,2:T(8,128)(2,1)S(1)} %fusion.8), channel_id=1, replica_groups=mesh['groups'=2,'sector'=4,'term'=2,'rep'=2] {'sector'}, dimensions={2} | all-to-all | bytes 524288 | tf_op jit(solution)/shard_map/all_to_all | solution.py:15
  281.3 9.3 %reduce-scatter.8.cloned.1.call-done = f32[4,1,256,128]{3,2,0,1:T(8,128)} async-done(((f32[4,1,256,256]{3,2,0,1:T(8,128)}), f32[4,1,256,128]{3,2,0,1:T(8,128)}) %reduce-scatter.8.cloned.1.call-update) | async-done | bytes 524304 | tf_op jit(solution)/shard_map/reduce_scatter | solution.py:19
  290.6 31.7 %all-reduce.9.cloned.1.call-done = f32[4,1,256,128]{3,2,0,1:T(8,128)} async-done(((f32[4,1,256,128]{3,2,0,1:T(8,128)}), f32[4,1,256,128]{3,2,0,1:T(8,128)}) %all-reduce.9.cloned.1.call-update) | async-done | bytes 524304 | tf_op jit(solution)/shard_map/psum | solution.py:20
  322.3 18.0 %all_to_all.68 = f32[4,1,256,128]{3,2,1,0:T(8,128)S(1)} all-to-all(f32[4,1,256,128]{3,2,1,0:T(8,128)} %bitcast.124), channel_id=1, replica_groups=mesh['groups'=2,'sector'=4,'term'=2,'rep'=2] {'sector'}, dimensions={0} | all-to-all | bytes 1048576 | tf_op jit(solution)/shard_map/all_to_all | solution.py:21
  (38 shorter events, 9.2 us)
Async XLA Ops:
  7.2 18.4 %copy-start = (bf16[1,1,4,256,256]{4,3,2,1,0:T(8,128)(2,1)S(1)}, bf16[1,1,4,256,256]{4,3,2,1,0:T(8,128)(2,1)}, u32[]{:S(2)}) copy-start(bf16[1,1,4,256,256]{4,3,2,1,0:T(8,128)(2,1)} %param.7) | copy-start | bytes 1572868
  7.2 18.4 %copy-start.1 = (bf16[1,4,256,128]{3,2,1,0:T(8,128)(2,1)S(1)}, bf16[1,4,256,128]{3,2,1,0:T(8,128)(2,1)}, u32[]{:S(2)}) copy-start(bf16[1,4,256,128]{3,2,1,0:T(8,128)(2,1)} %param.5) | copy-start | bytes 786436
  7.2 41.2 %reduce-scatter.4.cloned.1.call-start = ((), (), s32[]{:S(2)}) async-start(), calls=%async_computation.9 | async-start | bytes 1572864 | tf_op jit(solution)/shard_map/reduce_scatter | solution.py:19
  24.9 0.7 copy-start.5
  25.9 9.9 %copy-start.3 = (bf16[1,1,4,256,128]{4,3,2,1,0:T(8,128)(2,1)S(1)}, bf16[1,1,4,256,128]{4,3,2,1,0:T(8,128)(2,1)}, u32[]{:S(2)}) copy-start(bf16[1,1,4,256,128]{4,3,2,1,0:T(8,128)(2,1)} %param.8) | copy-start | bytes 786436
  37.1 43.1 %all-reduce.5.cloned.1.call-start = ((), (), s32[]{:S(2)}) async-start(), calls=%async_computation.10 | async-start | bytes 1048576 | tf_op jit(solution)/shard_map/psum | solution.py:20
  48.4 118.7 %reduce-scatter.6.cloned.1.call-start = ((), (), s32[]{:S(2)}) async-start(), calls=%async_computation.11 | async-start | bytes 1572864 | tf_op jit(solution)/shard_map/reduce_scatter | solution.py:19
  98.1 16.8 %copy-start.2 = (bf16[1,4,256,128]{3,2,1,0:T(8,128)(2,1)S(1)}, bf16[1,4,256,128]{3,2,1,0:T(8,128)(2,1)}, u32[]{:S(2)}) copy-start(bf16[1,4,256,128]{3,2,1,0:T(8,128)(2,1)} %param.6) | copy-start | bytes 786436
  157.7 41.0 %all-reduce.7.cloned.1.call-start = ((), (), s32[]{:S(2)}) async-start(), calls=%async_computation.12 | async-start | bytes 1048576 | tf_op jit(solution)/shard_map/psum | solution.py:20
  167.1 123.5 %reduce-scatter.8.cloned.1.call-start = ((), (), s32[]{:S(2)}) async-start(), calls=%async_computation.13 | async-start | bytes 1572864 | tf_op jit(solution)/shard_map/reduce_scatter | solution.py:19
  269.7 0.8 copy-start.4
  281.2 41.0 %all-reduce.9.cloned.1.call-start = ((), (), s32[]{:S(2)}) async-start(), calls=%async_computation.14 | async-start | bytes 1048576 | tf_op jit(solution)/shard_map/psum | solution.py:20
Sparse Core Ops, SparseCore 0:
  37.2 11.0 reduce-scatter.3
  50.7 29.3 all-reduce.4
  157.9 9.1 reduce-scatter.5
  169.3 29.3 all-reduce.6
  281.4 9.1 reduce-scatter.7
  292.8 29.3 all-reduce.8
where the time goes:
time: 351 us; the launch traced here: 349 us
  blocking collectives  186 us (53%)
  waiting for transfers between devices  125 us (36%)
  between operations  21.5 us (6%)
  other arithmetic  9.39 us (3%)
  matrix products  4.93 us (1%)
    psum x3, waiting for transfers between devices, apply_h(): totals = lax.psum(halves, 'term')  95 us
    all_to_all x3, blocking collectives, apply_h(): lax.all_to_all(totals, 'sector', split_axis=0, concat_axis=1, tiled=True)  53.9 us
    reduce_scatter x3, waiting for transfers between devices, apply_h(): lax.psum_scatter(partial_sums, 'rep', scatter_dimension=3, tiled=True)  29.8 us
    psum x2, blocking collectives, orthonormal(): coefs = lax.psum(local_terms, ('sector', 'rep')) / count  28.7 us
    all_to_all x3, blocking collectives, apply_h(): lax.all_to_all(mixed, 'sector', split_axis=2, concat_axis=1, tiled=True)  28.6 us
    psum x2, blocking collectives, orthonormal(): length = lax.psum(jnp.sum(rest * rest), ('sector', 'rep')) / count  28.4 us
    psum x1, blocking collectives, local(): lax.psum((jnp.sum(vone * sigma_zero), jnp.sum(vone * sigma_one)), ('secto...  15.4 us
    psum x1, blocking collectives, local(): theta = lax.psum(jnp.sum(vzero * sigma_zero), ('sector', 'rep')) / count  15.4 us
  transfers between devices with their start and end apart: 6, of which 6 were waited for; matrix products, arithmetic and copies ran while one was open for 0% of the time, Pallas kernels for 0%

commit v1 on v0

v1 whole, which is shorter than its diff:
```python
import functools
import jax
import jax.numpy as jnp
from jax import lax
from jax.experimental import pallas as pl
from jax.experimental.pallas import tpu as pltpu
from jax.sharding import PartitionSpec as P

eps = 1e-06
MESH = pl.DeviceIdType.MESH
f32 = jnp.float32
bf16 = jnp.bfloat16


def loop(low, high, body):
    if high - low <= 16:
        for k in range(low, high):
            body(k)
    else:
        lax.fori_loop(low, high, lambda k, c: (body(k), c)[1], 0)


def pack(sums):
    lane = lax.broadcasted_iota(jnp.int32, (1, 128), 1)
    row = jnp.zeros((1, 128), f32)
    for k, value in enumerate(sums):
        if value.shape != (1, 1):
            value = jnp.sum(value, axis=1, keepdims=True)
        row = row + jnp.where(lane == k, value, 0.0)
    return row


def partial(products):
    total = products[0]
    for other in products[1:]:
        total = total + other
    return jnp.sum(total, axis=0, keepdims=True)


def kernel(
    S, T, R, nj, count,
    v_in, p_in, l_in, r_in, used,
    nv_out, img_out, ritz_out,
    vloc, vbuf, pbuf, lbuf, rbuf, nvbuf, imgbuf, rows,
    local_sem, vsem, psem, lsem, rsem, row_sem, row_send, v_send, p_send, l_send, r_send,
    out_sem, out_send,
):
    N = S * T * R
    SB = nj * T * R
    B = lbuf.shape[-1]
    H = B // R
    s, t, r = lax.axis_index("sector"), lax.axis_index("term"), lax.axis_index("rep")
    me = (s * T + t) * R + r

    def device(rank):
        return {"sector": rank // (T * R), "term": lax.rem(rank // R, T), "rep": lax.rem(rank, R)}

    def first(t2, r2):
        return (t2 * R + r2) * nj

    def half(r2):
        return pl.ds(pl.multiple_of(r2 * H, H), H)

    own = pl.ds(first(t, r), nj)
    load = pltpu.make_async_copy(v_in.at[0, pl.ds(t * R * nj, R * nj)], vloc, local_sem)
    load.start()
    pltpu.make_async_copy(v_in.at[0, own], vbuf.at[:, :, half(r)], vsem).start()
    pltpu.make_async_copy(p_in.at[0, own], pbuf.at[:, :, half(r)], psem).start()
    pltpu.make_async_copy(l_in.at[0, 0, own], lbuf.at[t], lsem).start()

    barrier = pltpu.get_barrier_semaphore()

    def greet(k):
        pl.semaphore_signal(barrier, inc=1, device_id=device(lax.rem(me + k, N)), device_id_type=MESH)

    loop(1, N, greet)

    load.wait()
    lane = lax.broadcasted_iota(jnp.int32, (1, 128), 1)
    local_v = [vloc[k].astype(f32) for k in range(R * nj)]
    row = pack([partial([x * x for x in local_v])])
    for j in range(SB):
        row = row + jnp.where(lane == 8 + j, used[0, 0, j].astype(f32), 0.0)

    def send_row(index, row):
        rows[index, me] = row

        def one(k):
            peer = lax.rem(me + k, N)
            pltpu.make_async_remote_copy(
                rows.at[index, me], rows.at[index, me], row_send.at[index], row_sem.at[index],
                device_id=device(peer), device_id_type=MESH,
            ).start()

        loop(1, N, one)

    def wait_rows(index):
        some = rows.at[index, pl.ds(0, N - 1)]
        pltpu.make_async_copy(some, some, row_sem.at[index]).wait()
        return rows[index].reshape(N, 128)

    pl.semaphore_wait(barrier, N - 1)
    send_row(0, row)

    def v_copy(k, src, dst, sem, recv):
        r2 = lax.rem(r + k, R)
        return pltpu.make_async_remote_copy(
            src.at[0, pl.ds(first(t, r2), nj)], dst.at[:, :, half(r)], sem.at[k - 1], recv,
            device_id={"sector": s, "term": t, "rep": r2}, device_id_type=MESH,
        )

    def l_copy(k):
        t2 = lax.rem(t + k, T)
        return pltpu.make_async_remote_copy(
            l_in.at[0, 0, pl.ds(first(t2, r), nj)], lbuf.at[t], l_send.at[k - 1], lsem,
            device_id={"sector": s, "term": t2, "rep": r}, device_id_type=MESH,
        )

    owner = s // nj
    owner_t, owner_r, slot = owner // R, lax.rem(owner, R), lax.rem(s, nj)
    mine = jnp.logical_and(owner_t == t, owner_r == r)

    def r_copy(k):
        i2 = lax.rem(s + k, S)
        return pltpu.make_async_remote_copy(
            r_in.at[0, 0, i2], rbuf.at[t, slot, :, half(r)], r_send.at[k], rsem,
            device_id={"sector": i2, "term": owner_t, "rep": owner_r}, device_id_type=MESH,
        )

    loop(1, R, lambda k: v_copy(k, v_in, vbuf, v_send, vsem).start())
    loop(1, R, lambda k: v_copy(k, p_in, pbuf, p_send, psem).start())
    loop(1, S, lambda k: r_copy(k).start())

    @pl.when(mine)
    def _():
        pltpu.make_async_copy(r_in.at[0, 0, s], rbuf.at[t, slot, :, half(r)], rsem).start()

    @pl.when(jnp.logical_not(mine))
    def _():
        r_copy(0).start()

    loop(1, T, lambda k: l_copy(k).start())

    def whole(ref, sem):
        pltpu.make_async_copy(ref, ref, sem).wait()

    m0 = wait_rows(0)
    square = jnp.sum(m0[:, 0:1], axis=0, keepdims=True) / count
    scale = 1.0 / jnp.sqrt(square + eps)
    masks = []
    for t2 in range(T):
        peer_row = rows[0, (s * T + t2) * R + r]
        masks.append([
            jnp.sum(jnp.where(lane == 8 + first(t, r) + q, peer_row, 0.0), axis=1, keepdims=True)
            for q in range(nj)
        ])
    whole(vbuf, vsem)
    v0 = [vbuf[q].astype(f32) * scale for q in range(nj)]
    whole(pbuf, psem)
    ip = [1.0 / pbuf[q].astype(f32) for q in range(nj)]
    whole(lbuf, lsem)
    whole(rbuf, rsem)

    def apply_h(v):
        result = []
        for q in range(nj):
            rounded = v[q].astype(bf16)
            total = None
            for t2 in range(T):
                mixed = jnp.dot(lbuf[t2, q], rounded, preferred_element_type=f32)
                mixed = (mixed * masks[t2][q]).astype(bf16)
                piece = lax.dot_general(
                    mixed, rbuf[t2, q], (((1,), (1,)), ((), ())), preferred_element_type=f32
                )
                total = piece if total is None else total + piece
            result.append(total)
        return result

    def inner(x, y):
        return partial([a * b for a, b in zip(x, y)])

    def lanes(x):
        return jnp.sum(x, axis=1, keepdims=True)

    def columns(m, n):
        return [m[:, k:k + 1] for k in range(n)]

    def add(x):
        return jnp.sum(x, axis=0, keepdims=True) / count

    s0 = apply_h(v0)
    n_loc = lanes(inner(v0, v0))
    a_loc = lanes(inner(v0, s0))
    th_loc = a_loc / jnp.maximum(n_loc, 1e-30)
    bb = [a * b for a, b in zip(v0, ip)]
    tt = [(a - th_loc * b) * c for a, b, c in zip(s0, v0, ip)]
    send_row(1, pack([
        n_loc, a_loc, th_loc, inner(v0, tt), inner(v0, bb), inner(tt, tt), inner(tt, bb),
        inner(bb, bb), inner(tt, s0), inner(bb, s0),
    ]))
    n0, a0, th, vt, vb, t_t, t_b, b_b, ts, bs = columns(wait_rows(1), 10)
    theta = add(a0)
    delta = th - theta
    coef = add(vt + delta * vb)
    length = add(
        t_t + delta * (2.0 * t_b + delta * b_b) - coef * (2.0 * (vt + delta * vb) - coef * n0)
    )
    inv = 1.0 / jnp.sqrt(jnp.maximum(length, 0.0) + eps)
    cross = add(ts + delta * bs - coef * a0) * inv
    d_loc = th_loc - theta
    v1 = [(x + d_loc * y - coef * z) * inv for x, y, z in zip(tt, bb, v0)]

    s1 = apply_h(v1)
    xx = [(x - theta * y - cross * z) * w for x, y, z, w in zip(s0, v0, v1, ip)]
    zz = [x * y for x, y in zip(v1, ip)]
    n1_loc = lanes(inner(v1, v1))
    d1_loc = lanes(inner(v1, s1))
    g_loc = d1_loc / jnp.maximum(n1_loc, 1e-30)
    yy = [(x - cross * y - g_loc * z) * w for x, y, z, w in zip(s1, v0, v1, ip)]
    send_row(2, pack([
        n1_loc, d1_loc, g_loc, inner(v0, v1),
        inner(xx, xx), inner(xx, yy), inner(xx, zz), inner(yy, yy), inner(yy, zz), inner(zz, zz),
        inner(v0, xx), inner(v0, yy), inner(v0, zz), inner(v1, xx), inner(v1, yy), inner(v1, zz),
    ]))
    (n1, d1, g, o01, xx_, xy_, xz_, yy_, yz_, zz_, ax, ay, az, bx, by, bz) = columns(wait_rows(2), 16)
    diag = add(d1)
    gap = (theta - diag) * 0.5
    lowest = (theta + diag) * 0.5 - jnp.sqrt(gap * gap + cross * cross)
    size = jnp.sqrt(cross * cross + (lowest - theta) * (lowest - theta))
    c0 = cross / size
    c1 = (lowest - theta) / size
    e = c1 * (g - diag)
    f0d = c0 * ax + c1 * ay + e * az
    f1d = c0 * bx + c1 * by + e * bz
    f0 = add(f0d)
    f1 = add(f1d)
    square1 = (
        c0 * c0 * xx_ + c1 * c1 * yy_ + e * e * zz_
        + 2.0 * (c0 * c1 * xy_ + c0 * e * xz_ + c1 * e * yz_)
    )
    length1 = add(
        square1 - 2.0 * (f0 * f0d + f1 * f1d) + f0 * f0 * n0 + f1 * f1 * n1 + 2.0 * f0 * f1 * o01
    )
    inv1 = 1.0 / jnp.sqrt(jnp.maximum(length1, 0.0) + eps)
    e_loc = c1 * (g_loc - diag)
    v2 = []
    for q in range(nj):
        new = (c0 * xx[q] + c1 * yy[q] + e_loc * zz[q] - f0 * v0[q] - f1 * v1[q]) * inv1
        nvbuf[q] = new
        v2.append(new)

    def out_copy(k, src, dst, which):
        place = lax.rem(t * R + r + k, T * R)
        t2, r2 = place // R, lax.rem(place, R)
        if k == 0:
            return pltpu.make_async_copy(src.at[:, :, half(r2)], dst.at[0, own], out_sem.at[which])
        return pltpu.make_async_remote_copy(
            src.at[:, :, half(r2)], dst.at[0, own], out_send.at[which, k - 1], out_sem.at[which],
            device_id={"sector": s, "term": t2, "rep": r2}, device_id_type=MESH,
        )

    for k in range(T * R):
        out_copy(k, nvbuf, nv_out, 0).start()
    s2 = apply_h(v2)
    for q in range(nj):
        imgbuf[q] = s2[q]
    for k in range(T * R):
        out_copy(k, imgbuf, img_out, 1).start()
    ritz_out[0] = jnp.sum(lowest)

    for index in range(3):
        some = rows.at[index, pl.ds(0, N - 1)]
        pltpu.make_async_copy(some, some, row_send.at[index]).wait()
    loop(1, R, lambda k: v_copy(k, v_in, vbuf, v_send, vsem).wait_send())
    loop(1, R, lambda k: v_copy(k, p_in, pbuf, p_send, psem).wait_send())
    loop(1, S, lambda k: r_copy(k).wait_send())

    @pl.when(jnp.logical_not(mine))
    def _():
        r_copy(0).wait_send()

    loop(1, T, lambda k: l_copy(k).wait_send())
    for k in range(1, T * R):
        out_copy(k, nvbuf, nv_out, 0).wait_send()
        out_copy(k, imgbuf, img_out, 1).wait_send()
    whole(nv_out, out_sem.at[0])
    whole(img_out, out_sem.at[1])


def solution(mesh):
    S, T, R = mesh.shape["sector"], mesh.shape["term"], mesh.shape["rep"]

    def local(start_vector, precond, left_env, right_env, blocks_used):
        SB, B, H = start_vector.shape[1:]
        nj = SB // (T * R)
        N = S * T * R
        count = float(start_vector.size * S * R)
        dma = pltpu.SemaphoreType.DMA
        hbm = pl.BlockSpec(memory_space=pl.ANY)
        vmem = pl.BlockSpec(memory_space=pltpu.VMEM)
        smem = pl.BlockSpec(memory_space=pltpu.SMEM)
        shape = jax.ShapeDtypeStruct(start_vector.shape, f32)
        return tuple(pl.pallas_call(
            functools.partial(kernel, S, T, R, nj, count),
            out_shape=(shape, shape, jax.ShapeDtypeStruct((1,), f32)),
            in_specs=[hbm, hbm, hbm, hbm, smem],
            out_specs=(vmem, vmem, smem),
            scratch_shapes=[
                pltpu.VMEM((R * nj, B, H), bf16),
                pltpu.VMEM((nj, B, B), bf16),
                pltpu.VMEM((nj, B, B), bf16),
                pltpu.VMEM((T, nj, B, B), bf16),
                pltpu.VMEM((T, nj, B, B), bf16),
                pltpu.VMEM((nj, B, B), f32),
                pltpu.VMEM((nj, B, B), f32),
                pltpu.VMEM((3, N, 1, 128), f32),
                dma, dma, dma, dma, dma, dma((3,)), dma((3,)), dma((R,)), dma((R,)), dma((T,)),
                dma((S,)), dma((2,)), dma((2, T * R)),
            ],
            compiler_params=pltpu.CompilerParams(
                collective_id=0, has_side_effects=True, vmem_limit_bytes=40 * 2**20
            ),
            name="davidson",
        )(start_vector, precond, left_env, right_env, blocks_used))

    in_specs = (
        P(("groups", "sector"), None, None, "rep"),
        P(("groups", "sector"), None, None, "rep"),
        P("term", ("groups", "sector"), None, None, None),
        P("term", "sector", "groups", None, "rep"),
        P("term", ("groups", "sector"), None),
    )
    out_specs = (
        P(("groups", "sector"), None, None, "rep"),
        P(("groups", "sector"), None, None, "rep"),
        P("groups"),
    )
    return jax.shard_map(local, mesh=mesh, in_specs=in_specs, out_specs=out_specs, check_vma=False)
```

time: 351 us -> 46.5 us (0.13)
  blocking collectives: 186 us -> 0 us
  waiting for transfers between devices: 125 us -> 0 us
  Pallas kernels: 0 us -> 37.7 us
  between operations: 21.5 us -> 2.34 us
  other arithmetic: 9.39 us -> 0 us
  matrix products: 4.93 us -> 0 us
  local copies, waits for them, and re-layouts: 2.48 us -> 6.13 us
    psum x7 -> x0, blocking collectives: 103 us -> none  [the longest x2 28.7 us: orthonormal(): coefs = lax.psum(local_terms, ('sector', 'rep')) / count]
    psum x3 -> x0, waiting for transfers between devices: 95 us -> none  [apply_h(): totals = lax.psum(halves, 'term')]
    all_to_all x6 -> x0, blocking collectives: 82.5 us -> none  [the longest x3 53.9 us: apply_h(): lax.all_to_all(totals, 'sector', split_axis=0, concat_axis=1, tiled=True)]
    pallas_call x0 -> x1, Pallas kernels: none -> 37.7 us  [local(): pl.pallas_call(functools.partial(kernel, S, T, R, nj, count), out_shape=(...]
    reduce_scatter x3 -> x0, waiting for transfers between devices: 29.8 us -> none  [apply_h(): lax.psum_scatter(partial_sums, 'rep', scatter_dimension=3, tiled=True)]
    reduce_sum x7 -> x0, other arithmetic: 7.97 us -> none  [the longest x2 2.92 us: orthonormal(): length = lax.psum(jnp.sum(rest * rest), ('sector', 'rep')) / count]
    dot_general x6 -> x0, matrix products: 4.93 us -> none  [the longest x3 3.98 us: apply_h(): jnp.einsum('tijac,tjidc->ijad', lax.all_to_all(mixed, 'sector', split_axi...]
    unnamed x13 -> x12, local copies, waits for them, and re-layouts: 1.9 us -> 6.13 us
  transfers between devices with their start and end apart: 6 -> 0, of which waited for: 6 -> 0; matrix products, arithmetic and copies ran while one was open for 0% -> 0% of each run, Pallas kernels for 0% -> 0%
where the time goes in v1:
time: 46.5 us; the launch traced here: 46.2 us
  Pallas kernels  37.7 us (81%)
  local copies, waits for them, and re-layouts  6.13 us (13%)
  between operations  2.34 us (5%)
    pallas_call x1, Pallas kernels, local(): pl.pallas_call(functools.partial(kernel, S, T, R, nj, count), out_shape=(...  37.7 us
    unnamed x12, local copies, waits for them, and re-layouts  6.13 us

profile of v1, /device:TPU:1, one launch (start us, length us, event | category | flops | bytes accessed | tf_op | source)
XLA Modules:
  0.0 46.2 jit_solution(17235311170913327946)
XLA Ops:
  0.6 0.0 copy-start
  0.6 1.0 %copy-done = bf16[1,1,4,256,256]{4,3,2,1,0:T(8,128)(2,1)S(1)} copy-done((bf16[1,1,4,256,256]{4,3,2,1,0:T(8,128)(2,1)S(1)}, bf16[1,1,4,256,256]{4,3,2,1,0:T(8,128)(2,1)}, u32[]{:S(2)}) %copy-start) | copy-done | bytes 524312
  1.7 0.0 copy-start.1
  1.7 0.9 %copy-done.1 = bf16[1,4,256,128]{3,2,1,0:T(8,128)(2,1)S(1)} copy-done((bf16[1,4,256,128]{3,2,1,0:T(8,128)(2,1)S(1)}, bf16[1,4,256,128]{3,2,1,0:T(8,128)(2,1)}, u32[]{:S(2)}) %copy-start.1) | copy-done | bytes 262168
  2.6 0.0 copy-start.2
  2.6 0.9 %copy-done.2 = bf16[1,4,256,128]{3,2,1,0:T(8,128)(2,1)S(1)} copy-done((bf16[1,4,256,128]{3,2,1,0:T(8,128)(2,1)S(1)}, bf16[1,4,256,128]{3,2,1,0:T(8,128)(2,1)}, u32[]{:S(2)}) %copy-start.2) | copy-done | bytes 262168
  3.6 0.0 copy-start.3
  3.6 0.9 %copy-done.3 = bf16[1,1,4,256,128]{4,3,2,1,0:T(8,128)(2,1)S(1)} copy-done((bf16[1,1,4,256,128]{4,3,2,1,0:T(8,128)(2,1)S(1)}, bf16[1,1,4,256,128]{4,3,2,1,0:T(8,128)(2,1)}, u32[]{:S(2)}) %copy-start.3) | copy-done | bytes 262168
  4.5 0.0 copy-start.4
  4.5 0.7 %copy-done.4 = s32[1,1,4]{2,1,0:T(1,128)S(1)} copy-done((s32[1,1,4]{2,1,0:T(1,128)S(1)}, s32[1,1,4]{2,1,0:T(1,128)}, u32[]{:S(2)}) %copy-start.4) | copy-done | bytes 40
  5.2 37.7 %davidson.1 = (f32[1,4,256,128]{3,2,1,0:T(8,128)S(1)}, f32[1,4,256,128]{3,2,1,0:T(8,128)S(1)}, f32[1]{0:T(128)}) custom-call(bf16[1,4,256,128]{3,2,1,0:T(8,128)(2,1)S(1)} %copy-done.1, bf16[1,4,256,128]{3,2,1,0:T(8,128)(2,1)S(1)} %copy-done.2, bf16[1,1,4,256,256]{4,3,2,1,0:T(8,128)(2,1)S(1)} %copy-done, bf16[1,1,4,256,128]{4,3,2,1,0:T(8,128)(2,1)S(1)} %copy-done.3, ...), custom_call_target="tpu_custom_call" | custom-call | tf_op jit(solution)/shard_map/davidson/pallas_call | solution.py:303
  42.9 0.8 %copy.11 = f32[1,4,256,128]{3,2,1,0:T(8,128)} copy(f32[1,4,256,128]{3,2,1,0:T(8,128)S(1)} %get-tuple-element.6) | data formatting | bytes 1048576
  43.7 0.8 %copy.12 = f32[1,4,256,128]{3,2,1,0:T(8,128)} copy(f32[1,4,256,128]{3,2,1,0:T(8,128)S(1)} %get-tuple-element.7) | data formatting | bytes 1048576
Async XLA Ops:
  0.6 1.0 %copy-start = (bf16[1,1,4,256,256]{4,3,2,1,0:T(8,128)(2,1)S(1)}, bf16[1,1,4,256,256]{4,3,2,1,0:T(8,128)(2,1)}, u32[]{:S(2)}) copy-start(bf16[1,1,4,256,256]{4,3,2,1,0:T(8,128)(2,1)} %l_in.1) | copy-start | bytes 1572868
  1.7 0.9 %copy-start.1 = (bf16[1,4,256,128]{3,2,1,0:T(8,128)(2,1)S(1)}, bf16[1,4,256,128]{3,2,1,0:T(8,128)(2,1)}, u32[]{:S(2)}) copy-start(bf16[1,4,256,128]{3,2,1,0:T(8,128)(2,1)} %v_in.1) | copy-start | bytes 786436
  2.6 0.9 %copy-start.2 = (bf16[1,4,256,128]{3,2,1,0:T(8,128)(2,1)S(1)}, bf16[1,4,256,128]{3,2,1,0:T(8,128)(2,1)}, u32[]{:S(2)}) copy-start(bf16[1,4,256,128]{3,2,1,0:T(8,128)(2,1)} %p_in.1) | copy-start | bytes 786436
  3.6 0.9 %copy-start.3 = (bf16[1,1,4,256,128]{4,3,2,1,0:T(8,128)(2,1)S(1)}, bf16[1,1,4,256,128]{4,3,2,1,0:T(8,128)(2,1)}, u32[]{:S(2)}) copy-start(bf16[1,1,4,256,128]{4,3,2,1,0:T(8,128)(2,1)} %r_in.1) | copy-start | bytes 786436
  4.5 0.7 %copy-start.4 = (s32[1,1,4]{2,1,0:T(1,128)S(1)}, s32[1,1,4]{2,1,0:T(1,128)}, u32[]{:S(2)}) copy-start(s32[1,1,4]{2,1,0:T(1,128)} %used.1) | copy-start | bytes 52

commit v2 on v1

--- a/solution.py
+++ b/solution.py
@@ -246,7 +246,7 @@
     v2 = []
     for q in range(nj):
         new = (c0 * xx[q] + c1 * yy[q] + e_loc * zz[q] - f0 * v0[q] - f1 * v1[q]) * inv1
-        nvbuf[q] = new
+        nvbuf[q] = new.astype(bf16)
         v2.append(new)
 
     def out_copy(k, src, dst, which):
@@ -263,7 +263,7 @@
         out_copy(k, nvbuf, nv_out, 0).start()
     s2 = apply_h(v2)
     for q in range(nj):
-        imgbuf[q] = s2[q]
+        imgbuf[q] = s2[q].astype(bf16)
     for k in range(T * R):
         out_copy(k, imgbuf, img_out, 1).start()
     ritz_out[0] = jnp.sum(lowest)
@@ -296,11 +296,11 @@
         N = S * T * R
         count = float(start_vector.size * S * R)
         dma = pltpu.SemaphoreType.DMA
-        hbm = pl.BlockSpec(memory_space=pl.ANY)
+        hbm = pl.BlockSpec(memory_space=pltpu.HBM)
         vmem = pl.BlockSpec(memory_space=pltpu.VMEM)
         smem = pl.BlockSpec(memory_space=pltpu.SMEM)
-        shape = jax.ShapeDtypeStruct(start_vector.shape, f32)
-        return tuple(pl.pallas_call(
+        shape = jax.ShapeDtypeStruct(start_vector.shape, bf16)
+        vector, image, ritz = pl.pallas_call(
             functools.partial(kernel, S, T, R, nj, count),
             out_shape=(shape, shape, jax.ShapeDtypeStruct((1,), f32)),
             in_specs=[hbm, hbm, hbm, hbm, smem],
@@ -311,17 +311,18 @@
                 pltpu.VMEM((nj, B, B), bf16),
                 pltpu.VMEM((T, nj, B, B), bf16),
                 pltpu.VMEM((T, nj, B, B), bf16),
-                pltpu.VMEM((nj, B, B), f32),
-                pltpu.VMEM((nj, B, B), f32),
+                pltpu.VMEM((nj, B, B), bf16),
+                pltpu.VMEM((nj, B, B), bf16),
                 pltpu.VMEM((3, N, 1, 128), f32),
                 dma, dma, dma, dma, dma, dma((3,)), dma((3,)), dma((R,)), dma((R,)), dma((T,)),
                 dma((S,)), dma((2,)), dma((2, T * R)),
             ],
             compiler_params=pltpu.CompilerParams(
-                collective_id=0, has_side_effects=True, vmem_limit_bytes=40 * 2**20
+                collective_id=0, has_side_effects=True, vmem_limit_bytes=60 * 2**20
             ),
             name="davidson",
-        )(start_vector, precond, left_env, right_env, blocks_used))
+        )(start_vector, precond, left_env, right_env, blocks_used)
+        return vector.astype(f32), image.astype(f32), ritz
 
     in_specs = (
         P(("groups", "sector"), None, None, "rep"),

time: 46.5 us -> 37.6 us (0.81)
  local copies, waits for them, and re-layouts: 6.13 us -> 0.01 us
  Pallas kernels: 37.7 us -> 32.4 us
  other arithmetic: 0 us -> 2.65 us
    unnamed x12 -> x2, local copies, waits for them, and re-layouts: 6.13 us -> 0.01 us
    pallas_call x1, Pallas kernels: 37.7 us -> 32.4 us  [local(): pl.pallas_call(functools.partial(kernel, S, T, R, nj, count), out_shape=(...]
    convert_element_type x0 -> x2, other arithmetic: none -> 2.65 us  [local(): return (vector.astype(f32), image.astype(f32), ritz)]
where the time goes in v2:
time: 37.6 us; the launch traced here: 37.4 us
  Pallas kernels  32.4 us (86%)
  other arithmetic  2.65 us (7%)
  between operations  2.41 us (6%)
    pallas_call x1, Pallas kernels, local(): pl.pallas_call(functools.partial(kernel, S, T, R, nj, count), out_shape=(...  32.4 us
    convert_element_type x2, other arithmetic, local(): return (vector.astype(f32), image.astype(f32), ritz)  2.65 us

profile of v2, /device:TPU:1, one launch (start us, length us, event | category | flops | bytes accessed | tf_op | source)
XLA Modules:
  0.0 37.4 jit_solution(7892889841043072473)
XLA Ops:
  0.6 32.4 %davidson.1 = (bf16[1,4,256,128]{3,2,1,0:T(8,128)(2,1)}, bf16[1,4,256,128]{3,2,1,0:T(8,128)(2,1)}, f32[1]{0:T(128)}) custom-call(bf16[1,4,256,128]{3,2,1,0:T(8,128)(2,1)} %v_in.1, bf16[1,4,256,128]{3,2,1,0:T(8,128)(2,1)} %p_in.1, bf16[1,1,4,256,256]{4,3,2,1,0:T(8,128)(2,1)} %l_in.1, bf16[1,1,4,256,128]{4,3,2,1,0:T(8,128)(2,1)} %r_in.1, s32[1,1,4]{2,1,0:T(1,128)} %used.1), custom_call_target="tpu_custom_call" | custom-call | tf_op jit(solution)/shard_map/davidson/pallas_call | solution.py:303
  33.0 0.0 copy-start
  33.0 1.8 %convert_element_type.6 = f32[1,4,256,128]{3,2,1,0:T(8,128)} convert(bf16[1,4,256,128]{3,2,1,0:T(8,128)(2,1)} %get-tuple-element.6) | non-fusion elementwise | flops 131072 | bytes 786432 | tf_op jit(solution)/shard_map/convert_element_type | solution.py:325
  34.8 0.0 copy-done
  34.8 0.8 %convert_element_type.7 = f32[1,4,256,128]{3,2,1,0:T(8,128)} convert(bf16[1,4,256,128]{3,2,1,0:T(8,128)(2,1)S(1)} %copy-done) | non-fusion elementwise | flops 131072 | bytes 786432 | tf_op jit(solution)/shard_map/convert_element_type | solution.py:325
Async XLA Ops:
  33.0 1.8 %copy-start = (bf16[1,4,256,128]{3,2,1,0:T(8,128)(2,1)S(1)}, bf16[1,4,256,128]{3,2,1,0:T(8,128)(2,1)}, u32[]{:S(2)}) copy-start(bf16[1,4,256,128]{3,2,1,0:T(8,128)(2,1)} %get-tuple-element.7) | copy-start | bytes 786436

commit v3 on v2

--- a/solution.py
+++ b/solution.py
@@ -55,25 +55,42 @@
     def device(rank):
         return {"sector": rank // (T * R), "term": lax.rem(rank // R, T), "rep": lax.rem(rank, R)}
 
+    order = [a for a in (S - 1, 1) if 0 < a] if S > 1 else []
+    order = list(dict.fromkeys(order + list(range(2, S - 1)))) + [0]
+    peers = [(a, b, c) for a in order for b in reversed(range(T)) for c in reversed(range(R))][:-1]
+
+    def each_peer(body):
+        if N <= 16:
+            for a, b, c in peers:
+                body({"sector": lax.rem(s + a, S), "term": lax.rem(t + b, T), "rep": lax.rem(r + c, R)})
+        else:
+            lax.fori_loop(1, N, lambda k, c: (body(device(lax.rem(me + k, N))), c)[1], 0)
+
     def first(t2, r2):
         return (t2 * R + r2) * nj
 
     def half(r2):
         return pl.ds(pl.multiple_of(r2 * H, H), H)
+
+    C = B // 2
+    tiles = ((pl.ds(C, C), pl.ds(0, B)), (pl.ds(0, C), pl.ds(0, C)))
 
     own = pl.ds(first(t, r), nj)
     load = pltpu.make_async_copy(v_in.at[0, pl.ds(t * R * nj, R * nj)], vloc, local_sem)
     load.start()
     pltpu.make_async_copy(v_in.at[0, own], vbuf.at[:, :, half(r)], vsem).start()
     pltpu.make_async_copy(p_in.at[0, own], pbuf.at[:, :, half(r)], psem).start()
-    pltpu.make_async_copy(l_in.at[0, 0, own], lbuf.at[t], lsem).start()
+    for rows_of, lanes_of in tiles:
+        pltpu.make_async_copy(
+            l_in.at[0, 0, own, rows_of, lanes_of], lbuf.at[t, :, rows_of, lanes_of], lsem
+        ).start()
 
     barrier = pltpu.get_barrier_semaphore()
 
-    def greet(k):
-        pl.semaphore_signal(barrier, inc=1, device_id=device(lax.rem(me + k, N)), device_id_type=MESH)
-
-    loop(1, N, greet)
+    def greet(peer):
+        pl.semaphore_signal(barrier, inc=1, device_id=peer, device_id_type=MESH)
+
+    each_peer(greet)
 
     load.wait()
     lane = lax.broadcasted_iota(jnp.int32, (1, 128), 1)
@@ -85,14 +102,13 @@
     def send_row(index, row):
         rows[index, me] = row
 
-        def one(k):
-            peer = lax.rem(me + k, N)
+        def one(peer):
             pltpu.make_async_remote_copy(
                 rows.at[index, me], rows.at[index, me], row_send.at[index], row_sem.at[index],
-                device_id=device(peer), device_id_type=MESH,
+                device_id=peer, device_id_type=MESH,
             ).start()
 
-        loop(1, N, one)
+        each_peer(one)
 
     def wait_rows(index):
         some = rows.at[index, pl.ds(0, N - 1)]
@@ -109,10 +125,12 @@
             device_id={"sector": s, "term": t, "rep": r2}, device_id_type=MESH,
         )
 
-    def l_copy(k):
+    def l_copy(k, which):
         t2 = lax.rem(t + k, T)
+        rows_of, lanes_of = tiles[which]
         return pltpu.make_async_remote_copy(
-            l_in.at[0, 0, pl.ds(first(t2, r), nj)], lbuf.at[t], l_send.at[k - 1], lsem,
+            l_in.at[0, 0, pl.ds(first(t2, r), nj), rows_of, lanes_of],
+            lbuf.at[t, :, rows_of, lanes_of], l_send.at[k - 1, which], lsem,
             device_id={"sector": s, "term": t2, "rep": r}, device_id_type=MESH,
         )
 
@@ -120,26 +138,41 @@
     owner_t, owner_r, slot = owner // R, lax.rem(owner, R), lax.rem(s, nj)
     mine = jnp.logical_and(owner_t == t, owner_r == r)
 
-    def r_copy(k):
+    def r_copy(k, rows_of):
         i2 = lax.rem(s + k, S)
         return pltpu.make_async_remote_copy(
-            r_in.at[0, 0, i2], rbuf.at[t, slot, :, half(r)], r_send.at[k], rsem,
+            r_in.at[0, 0, i2, rows_of], rbuf.at[t, slot, rows_of, half(r)], r_send.at[k], rsem,
             device_id={"sector": i2, "term": owner_t, "rep": owner_r}, device_id_type=MESH,
         )
 
     loop(1, R, lambda k: v_copy(k, v_in, vbuf, v_send, vsem).start())
     loop(1, R, lambda k: v_copy(k, p_in, pbuf, p_send, psem).start())
-    loop(1, S, lambda k: r_copy(k).start())
-
-    @pl.when(mine)
-    def _():
-        pltpu.make_async_copy(r_in.at[0, 0, s], rbuf.at[t, slot, :, half(r)], rsem).start()
-
-    @pl.when(jnp.logical_not(mine))
-    def _():
-        r_copy(0).start()
-
-    loop(1, T, lambda k: l_copy(k).start())
+    def right(rows_of, finish):
+        for k in order[:-1]:
+            copy = r_copy(k, rows_of)
+            copy.wait_send() if finish else copy.start()
+
+        if not finish:
+
+            @pl.when(mine)
+            def _():
+                pltpu.make_async_copy(
+                    r_in.at[0, 0, s, rows_of], rbuf.at[t, slot, rows_of, half(r)], rsem
+                ).start()
+
+        @pl.when(jnp.logical_not(mine))
+        def _():
+            copy = r_copy(0, rows_of)
+            copy.wait_send() if finish else copy.start()
+
+    def both_halves(finish):
+        pl.when(r == 0)(lambda: right(pl.ds(0, B), finish))
+        pl.when(r != 0)(lambda: right(pl.ds(C, C), finish))
+
+    both_halves(False)
+
+    loop(1, T, lambda k: l_copy(k, 0).start())
+    loop(1, T, lambda k: l_copy(k, 1).start())
 
     def whole(ref, sem):
         pltpu.make_async_copy(ref, ref, sem).wait()
@@ -158,8 +191,12 @@
     v0 = [vbuf[q].astype(f32) * scale for q in range(nj)]
     whole(pbuf, psem)
     ip = [1.0 / pbuf[q].astype(f32) for q in range(nj)]
-    whole(lbuf, lsem)
-    whole(rbuf, rsem)
+    whole(lbuf.at[:, :, pl.ds(0, 3 * B // 4)], lsem)
+    whole(rbuf.at[:, :, pl.ds(0, 3 * B // 4)], rsem)
+    for buf in (lbuf, rbuf):
+        for t2 in range(T):
+            for q in range(nj):
+                buf[t2, q, 0:C, C:B] = buf[t2, q, C:B, 0:C].T
 
     def apply_h(v):
         result = []
@@ -273,18 +310,34 @@
         pltpu.make_async_copy(some, some, row_send.at[index]).wait()
     loop(1, R, lambda k: v_copy(k, v_in, vbuf, v_send, vsem).wait_send())
     loop(1, R, lambda k: v_copy(k, p_in, pbuf, p_send, psem).wait_send())
-    loop(1, S, lambda k: r_copy(k).wait_send())
-
-    @pl.when(jnp.logical_not(mine))
-    def _():
-        r_copy(0).wait_send()
-
-    loop(1, T, lambda k: l_copy(k).wait_send())
+    both_halves(True)
+    loop(1, T, lambda k: l_copy(k, 0).wait_send())
+    loop(1, T, lambda k: l_copy(k, 1).wait_send())
     for k in range(1, T * R):
         out_copy(k, nvbuf, nv_out, 0).wait_send()
         out_copy(k, imgbuf, img_out, 1).wait_send()
     whole(nv_out, out_sem.at[0])
     whole(img_out, out_sem.at[1])
+
+
+def widen(a_in, b_in, a_out, b_out, a_buf, b_buf, a_wide, b_wide, load_sem, store_sem):
+    sets = ((a_in, a_buf, a_wide, a_out), (b_in, b_buf, b_wide, b_out))
+    places = [(w, j) for j in range(a_buf.shape[0]) for w in range(2)]
+
+    def load(w, j):
+        return pltpu.make_async_copy(sets[w][0].at[0, j], sets[w][1].at[j], load_sem.at[w, j])
+
+    def store(w, j):
+        return pltpu.make_async_copy(sets[w][2].at[j], sets[w][3].at[0, j], store_sem.at[w, j])
+
+    for place in places:
+        load(*place).start()
+    for w, j in places:
+        load(w, j).wait()
+        sets[w][2][j] = sets[w][1][j].astype(f32)
+        store(w, j).start()
+    for place in places:
+        store(*place).wait()
 
 
 def solution(mesh):
@@ -314,7 +367,7 @@
                 pltpu.VMEM((nj, B, B), bf16),
                 pltpu.VMEM((nj, B, B), bf16),
                 pltpu.VMEM((3, N, 1, 128), f32),
-                dma, dma, dma, dma, dma, dma((3,)), dma((3,)), dma((R,)), dma((R,)), dma((T,)),
+                dma, dma, dma, dma, dma, dma((3,)), dma((3,)), dma((R,)), dma((R,)), dma((T, 2)),
                 dma((S,)), dma((2,)), dma((2, T * R)),
             ],
             compiler_params=pltpu.CompilerParams(
@@ -322,7 +375,21 @@
             ),
             name="davidson",
         )(start_vector, precond, left_env, right_env, blocks_used)
-        return vector.astype(f32), image.astype(f32), ritz
+        wide = jax.ShapeDtypeStruct(start_vector.shape, f32)
+        vector, image = pl.pallas_call(
+            widen,
+            out_shape=(wide, wide),
+            in_specs=[hbm, hbm],
+            out_specs=(hbm, hbm),
+            scratch_shapes=[
+                pltpu.VMEM((SB, B, H), bf16), pltpu.VMEM((SB, B, H), bf16),
+                pltpu.VMEM((SB, B, H), f32), pltpu.VMEM((SB, B, H), f32),
+                dma((2, SB)), dma((2, SB)),
+            ],
+            compiler_params=pltpu.CompilerParams(vmem_limit_bytes=60 * 2**20),
+            name="widen",
+        )(vector, image)
+        return vector, image, ritz
 
     in_specs = (
         P(("groups", "sector"), None, None, "rep"),

time: 37.6 us -> 35.5 us (0.944)
  other arithmetic: 2.65 us -> 0 us
  Pallas kernels: 32.4 us -> 32.9 us
    convert_element_type x2 -> x0, other arithmetic: 2.65 us -> none  [local(): return (vector.astype(f32), image.astype(f32), ritz)]
    pallas_call x0 -> x1, Pallas kernels: none -> 1.94 us  [local(): pl.pallas_call(widen, out_shape=(wide, wide), in_specs=[hbm, hbm], out_sp...]
    pallas_call x1, Pallas kernels: 32.4 us -> 30.9 us  [local(): pl.pallas_call(functools.partial(kernel, S, T, R, nj, count), out_shape=(...]
where the time goes in v3:
time: 35.5 us; the launch traced here: 35.3 us
  Pallas kernels  32.9 us (93%)
  between operations  2.41 us (7%)
    pallas_call x1, Pallas kernels, local(): pl.pallas_call(functools.partial(kernel, S, T, R, nj, count), out_shape=(...  30.9 us
    pallas_call x1, Pallas kernels, local(): pl.pallas_call(widen, out_shape=(wide, wide), in_specs=[hbm, hbm], out_sp...  1.94 us

profile of v3, /device:TPU:1, one launch (start us, length us, event | category | flops | bytes accessed | tf_op | source)
XLA Modules:
  0.0 35.3 jit_solution(3282132730704227938)
XLA Ops:
  0.6 30.9 %davidson.1 = (bf16[1,4,256,128]{3,2,1,0:T(8,128)(2,1)}, bf16[1,4,256,128]{3,2,1,0:T(8,128)(2,1)}, f32[1]{0:T(128)}) custom-call(bf16[1,4,256,128]{3,2,1,0:T(8,128)(2,1)} %v_in.1, bf16[1,4,256,128]{3,2,1,0:T(8,128)(2,1)} %p_in.1, bf16[1,1,4,256,256]{4,3,2,1,0:T(8,128)(2,1)} %l_in.1, bf16[1,1,4,256,128]{4,3,2,1,0:T(8,128)(2,1)} %r_in.1, s32[1,1,4]{2,1,0:T(1,128)} %used.1), custom_call_target="tpu_custom_call" | custom-call | tf_op jit(solution)/shard_map/davidson/pallas_call | solution.py:356
  31.6 1.9 %widen.1 = (f32[1,4,256,128]{3,2,1,0:T(8,128)}, f32[1,4,256,128]{3,2,1,0:T(8,128)}) custom-call(bf16[1,4,256,128]{3,2,1,0:T(8,128)(2,1)} %get-tuple-element.8.a_in, bf16[1,4,256,128]{3,2,1,0:T(8,128)(2,1)} %get-tuple-element.9.b_in), custom_call_target="tpu_custom_call" | custom-call | tf_op jit(solution)/shard_map/widen/pallas_call | solution.py:379

commit v4 on v3

--- a/solution.py
+++ b/solution.py
@@ -41,9 +41,9 @@
     S, T, R, nj, count,
     v_in, p_in, l_in, r_in, used,
     nv_out, img_out, ritz_out,
-    vloc, vbuf, pbuf, lbuf, rbuf, nvbuf, imgbuf, rows,
+    vloc, ploc, vbuf, pbuf, lbuf, rbuf, s0buf, s1buf, imgbuf, s0in, s1in, nvbuf, rows,
     local_sem, vsem, psem, lsem, rsem, row_sem, row_send, v_send, p_send, l_send, r_send,
-    out_sem, out_send,
+    out_sem, out_send, ploc_sem, nv_sem,
 ):
     N = S * T * R
     SB = nj * T * R
@@ -76,7 +76,7 @@
     tiles = ((pl.ds(C, C), pl.ds(0, B)), (pl.ds(0, C), pl.ds(0, C)))
 
     own = pl.ds(first(t, r), nj)
-    load = pltpu.make_async_copy(v_in.at[0, pl.ds(t * R * nj, R * nj)], vloc, local_sem)
+    load = pltpu.make_async_copy(v_in.at[0], vloc, local_sem)
     load.start()
     pltpu.make_async_copy(v_in.at[0, own], vbuf.at[:, :, half(r)], vsem).start()
     pltpu.make_async_copy(p_in.at[0, own], pbuf.at[:, :, half(r)], psem).start()
@@ -94,7 +94,7 @@
 
     load.wait()
     lane = lax.broadcasted_iota(jnp.int32, (1, 128), 1)
-    local_v = [vloc[k].astype(f32) for k in range(R * nj)]
+    local_v = [vloc[t * R * nj + k].astype(f32) for k in range(R * nj)]
     row = pack([partial([x * x for x in local_v])])
     for j in range(SB):
         row = row + jnp.where(lane == 8 + j, used[0, 0, j].astype(f32), 0.0)
@@ -117,6 +117,9 @@
 
     pl.semaphore_wait(barrier, N - 1)
     send_row(0, row)
+
+    p_load = pltpu.make_async_copy(p_in.at[0], ploc, ploc_sem)
+    p_load.start()
 
     def v_copy(k, src, dst, sem, recv):
         r2 = lax.rem(r + k, R)
@@ -225,6 +228,25 @@
     def add(x):
         return jnp.sum(x, axis=0, keepdims=True) / count
 
+    def out_copy(k, src, dst, which):
+        place = lax.rem(t * R + r + k, T * R)
+        t2, r2 = place // R, lax.rem(place, R)
+        if k == 0:
+            return pltpu.make_async_copy(src.at[:, :, half(r2)], dst.at[own], out_sem.at[which])
+        return pltpu.make_async_remote_copy(
+            src.at[:, :, half(r2)], dst.at[own], out_send.at[which, k - 1], out_sem.at[which],
+            device_id={"sector": s, "term": t2, "rep": r2}, device_id_type=MESH,
+        )
+
+    sent = ((s0buf, s0in), (s1buf, s1in), (imgbuf, img_out.at[0]))
+
+    def spread(which, value):
+        src, dst = sent[which]
+        for q in range(nj):
+            src[q] = value[q].astype(src.dtype)
+        for k in range(T * R):
+            out_copy((k + 1) % (T * R), src, dst, which).start()
+
     s0 = apply_h(v0)
     n_loc = lanes(inner(v0, v0))
     a_loc = lanes(inner(v0, s0))
@@ -235,6 +257,7 @@
         n_loc, a_loc, th_loc, inner(v0, tt), inner(v0, bb), inner(tt, tt), inner(tt, bb),
         inner(bb, bb), inner(tt, s0), inner(bb, s0),
     ]))
+    spread(0, s0)
     n0, a0, th, vt, vb, t_t, t_b, b_b, ts, bs = columns(wait_rows(1), 10)
     theta = add(a0)
     delta = th - theta
@@ -259,6 +282,7 @@
         inner(xx, xx), inner(xx, yy), inner(xx, zz), inner(yy, yy), inner(yy, zz), inner(zz, zz),
         inner(v0, xx), inner(v0, yy), inner(v0, zz), inner(v1, xx), inner(v1, yy), inner(v1, zz),
     ]))
+    spread(1, s1)
     (n1, d1, g, o01, xx_, xy_, xz_, yy_, yz_, zz_, ax, ay, az, bx, by, bz) = columns(wait_rows(2), 16)
     diag = add(d1)
     gap = (theta - diag) * 0.5
@@ -283,26 +307,24 @@
     v2 = []
     for q in range(nj):
         new = (c0 * xx[q] + c1 * yy[q] + e_loc * zz[q] - f0 * v0[q] - f1 * v1[q]) * inv1
-        nvbuf[q] = new.astype(bf16)
         v2.append(new)
 
-    def out_copy(k, src, dst, which):
-        place = lax.rem(t * R + r + k, T * R)
-        t2, r2 = place // R, lax.rem(place, R)
-        if k == 0:
-            return pltpu.make_async_copy(src.at[:, :, half(r2)], dst.at[0, own], out_sem.at[which])
-        return pltpu.make_async_remote_copy(
-            src.at[:, :, half(r2)], dst.at[0, own], out_send.at[which, k - 1], out_sem.at[which],
-            device_id={"sector": s, "term": t2, "rep": r2}, device_id_type=MESH,
-        )
-
-    for k in range(T * R):
-        out_copy(k, nvbuf, nv_out, 0).start()
     s2 = apply_h(v2)
-    for q in range(nj):
-        imgbuf[q] = s2[q].astype(bf16)
-    for k in range(T * R):
-        out_copy(k, imgbuf, img_out, 1).start()
+    spread(2, s2)
+
+    p_load.wait()
+    whole(s0in, out_sem.at[0])
+    whole(s1in, out_sem.at[1])
+    for j in range(SB):
+        v0_j = vloc[j].astype(f32) * scale
+        ip_j = 1.0 / ploc[j].astype(f32)
+        s0_j, s1_j = s0in[j], s1in[j].astype(f32)
+        r0_j = s0_j - theta * v0_j
+        v1_j = (r0_j * ip_j - coef * v0_j) * inv
+        r1_j = c0 * (r0_j - cross * v1_j) + c1 * (s1_j - cross * v0_j - diag * v1_j)
+        nvbuf[j] = (r1_j * ip_j - f0 * v0_j - f1 * v1_j) * inv1
+    nv_store = pltpu.make_async_copy(nvbuf, nv_out.at[0], nv_sem)
+    nv_store.start()
     ritz_out[0] = jnp.sum(lowest)
 
     for index in range(3):
@@ -313,15 +335,15 @@
     both_halves(True)
     loop(1, T, lambda k: l_copy(k, 0).wait_send())
     loop(1, T, lambda k: l_copy(k, 1).wait_send())
-    for k in range(1, T * R):
-        out_copy(k, nvbuf, nv_out, 0).wait_send()
-        out_copy(k, imgbuf, img_out, 1).wait_send()
-    whole(nv_out, out_sem.at[0])
-    whole(img_out, out_sem.at[1])
-
-
-def widen(a_in, b_in, a_out, b_out, a_buf, b_buf, a_wide, b_wide, load_sem, store_sem):
-    sets = ((a_in, a_buf, a_wide, a_out), (b_in, b_buf, b_wide, b_out))
+    for which, (src, dst) in enumerate(sent):
+        for k in range(1, T * R):
+            out_copy(k, src, dst, which).wait_send()
+    whole(img_out.at[0], out_sem.at[2])
+    nv_store.wait()
+
+
+def widen(a_in, b_in, a_out, b_out, a_buf, b_buf, b_wide, load_sem, store_sem):
+    sets = ((a_in, a_buf, a_buf, a_out), (b_in, b_buf, b_wide, b_out))
     places = [(w, j) for j in range(a_buf.shape[0]) for w in range(2)]
 
     def load(w, j):
@@ -334,7 +356,8 @@
         load(*place).start()
     for w, j in places:
         load(w, j).wait()
-        sets[w][2][j] = sets[w][1][j].astype(f32)
+        if w == 1:
+            b_wide[j] = b_buf[j].astype(f32)
         store(w, j).start()
     for place in places:
         store(*place).wait()
@@ -350,40 +373,44 @@
         count = float(start_vector.size * S * R)
         dma = pltpu.SemaphoreType.DMA
         hbm = pl.BlockSpec(memory_space=pltpu.HBM)
-        vmem = pl.BlockSpec(memory_space=pltpu.VMEM)
         smem = pl.BlockSpec(memory_space=pltpu.SMEM)
         shape = jax.ShapeDtypeStruct(start_vector.shape, bf16)
+        wide = jax.ShapeDtypeStruct(start_vector.shape, f32)
         vector, image, ritz = pl.pallas_call(
             functools.partial(kernel, S, T, R, nj, count),
-            out_shape=(shape, shape, jax.ShapeDtypeStruct((1,), f32)),
+            out_shape=(wide, shape, jax.ShapeDtypeStruct((1,), f32)),
             in_specs=[hbm, hbm, hbm, hbm, smem],
-            out_specs=(vmem, vmem, smem),
+            out_specs=(hbm, hbm, smem),
             scratch_shapes=[
-                pltpu.VMEM((R * nj, B, H), bf16),
+                pltpu.VMEM((SB, B, H), bf16),
+                pltpu.VMEM((SB, B, H), bf16),
                 pltpu.VMEM((nj, B, B), bf16),
                 pltpu.VMEM((nj, B, B), bf16),
                 pltpu.VMEM((T, nj, B, B), bf16),
                 pltpu.VMEM((T, nj, B, B), bf16),
+                pltpu.VMEM((nj, B, B), f32),
                 pltpu.VMEM((nj, B, B), bf16),
                 pltpu.VMEM((nj, B, B), bf16),
+                pltpu.VMEM((SB, B, H), f32),
+                pltpu.VMEM((SB, B, H), bf16),
+                pltpu.VMEM((SB, B, H), f32),
                 pltpu.VMEM((3, N, 1, 128), f32),
                 dma, dma, dma, dma, dma, dma((3,)), dma((3,)), dma((R,)), dma((R,)), dma((T, 2)),
-                dma((S,)), dma((2,)), dma((2, T * R)),
+                dma((S,)), dma((3,)), dma((3, T * R)), dma, dma,
             ],
             compiler_params=pltpu.CompilerParams(
                 collective_id=0, has_side_effects=True, vmem_limit_bytes=60 * 2**20
             ),
             name="davidson",
         )(start_vector, precond, left_env, right_env, blocks_used)
-        wide = jax.ShapeDtypeStruct(start_vector.shape, f32)
         vector, image = pl.pallas_call(
             widen,
             out_shape=(wide, wide),
             in_specs=[hbm, hbm],
             out_specs=(hbm, hbm),
             scratch_shapes=[
-                pltpu.VMEM((SB, B, H), bf16), pltpu.VMEM((SB, B, H), bf16),
-                pltpu.VMEM((SB, B, H), f32), pltpu.VMEM((SB, B, H), f32),
+                pltpu.VMEM((SB, B, H), f32), pltpu.VMEM((SB, B, H), bf16),
+                pltpu.VMEM((SB, B, H), f32),
                 dma((2, SB)), dma((2, SB)),
             ],
             compiler_params=pltpu.CompilerParams(vmem_limit_bytes=60 * 2**20),

time: 35.5 us -> 33 us (0.930)
  Pallas kernels: 32.9 us -> 30.4 us
    pallas_call x1, Pallas kernels: 30.9 us -> 28.4 us  [local(): pl.pallas_call(functools.partial(kernel, S, T, R, nj, count), out_shape=(...]
where the time goes in v4:
time: 33 us; the launch traced here: 32.9 us
  Pallas kernels  30.4 us (92%)
  between operations  2.41 us (7%)
    pallas_call x1, Pallas kernels, local(): pl.pallas_call(functools.partial(kernel, S, T, R, nj, count), out_shape=(...  28.4 us
    pallas_call x1, Pallas kernels, local(): pl.pallas_call(widen, out_shape=(wide, wide), in_specs=[hbm, hbm], out_sp...  2.02 us

profile of v4, /device:TPU:1, one launch (start us, length us, event | category | flops | bytes accessed | tf_op | source)
XLA Modules:
  0.0 32.9 jit_solution(6432034670190926115)
XLA Ops:
  0.6 28.4 %davidson.1 = (f32[1,4,256,128]{3,2,1,0:T(8,128)}, bf16[1,4,256,128]{3,2,1,0:T(8,128)(2,1)}, f32[1]{0:T(128)}) custom-call(bf16[1,4,256,128]{3,2,1,0:T(8,128)(2,1)} %v_in.1, bf16[1,4,256,128]{3,2,1,0:T(8,128)(2,1)} %p_in.1, bf16[1,1,4,256,256]{4,3,2,1,0:T(8,128)(2,1)} %l_in.1, bf16[1,1,4,256,128]{4,3,2,1,0:T(8,128)(2,1)} %r_in.1, s32[1,1,4]{2,1,0:T(1,128)} %used.1), custom_call_target="tpu_custom_call" | custom-call | tf_op jit(solution)/shard_map/davidson/pallas_call | solution.py:379
  29.1 2.0 %widen.1 = (f32[1,4,256,128]{3,2,1,0:T(8,128)}, f32[1,4,256,128]{3,2,1,0:T(8,128)}) custom-call(f32[1,4,256,128]{3,2,1,0:T(8,128)} %get-tuple-element.8.a_in, bf16[1,4,256,128]{3,2,1,0:T(8,128)(2,1)} %get-tuple-element.9.b_in), custom_call_target="tpu_custom_call" | custom-call | tf_op jit(solution)/shard_map/widen/pallas_call | solution.py:406

commit v5 on v4

--- a/solution.py
+++ b/solution.py
@@ -149,7 +149,8 @@
         )
 
     loop(1, R, lambda k: v_copy(k, v_in, vbuf, v_send, vsem).start())
-    loop(1, R, lambda k: v_copy(k, p_in, pbuf, p_send, psem).start())
+    loop(1, T, lambda k: l_copy(k, 0).start())
+    loop(1, T, lambda k: l_copy(k, 1).start())
     def right(rows_of, finish):
         for k in order[:-1]:
             copy = r_copy(k, rows_of)
@@ -174,8 +175,7 @@
 
     both_halves(False)
 
-    loop(1, T, lambda k: l_copy(k, 0).start())
-    loop(1, T, lambda k: l_copy(k, 1).start())
+    loop(1, R, lambda k: v_copy(k, p_in, pbuf, p_send, psem).start())
 
     def whole(ref, sem):
         pltpu.make_async_copy(ref, ref, sem).wait()
@@ -192,29 +192,39 @@
         ])
     whole(vbuf, vsem)
     v0 = [vbuf[q].astype(f32) * scale for q in range(nj)]
-    whole(pbuf, psem)
-    ip = [1.0 / pbuf[q].astype(f32) for q in range(nj)]
     whole(lbuf.at[:, :, pl.ds(0, 3 * B // 4)], lsem)
-    whole(rbuf.at[:, :, pl.ds(0, 3 * B // 4)], rsem)
-    for buf in (lbuf, rbuf):
+
+    def complete(buf):
         for t2 in range(T):
             for q in range(nj):
                 buf[t2, q, 0:C, C:B] = buf[t2, q, C:B, 0:C].T
 
-    def apply_h(v):
+    complete(lbuf)
+
+    def mix(v):
         result = []
         for q in range(nj):
             rounded = v[q].astype(bf16)
+            for t2 in range(T):
+                mixed = jnp.dot(lbuf[t2, q], rounded, preferred_element_type=f32)
+                result.append((mixed * masks[t2][q]).astype(bf16))
+        return result
+
+    def finish(mixed):
+        result = []
+        for q in range(nj):
             total = None
             for t2 in range(T):
-                mixed = jnp.dot(lbuf[t2, q], rounded, preferred_element_type=f32)
-                mixed = (mixed * masks[t2][q]).astype(bf16)
                 piece = lax.dot_general(
-                    mixed, rbuf[t2, q], (((1,), (1,)), ((), ())), preferred_element_type=f32
+                    mixed[q * T + t2], rbuf[t2, q], (((1,), (1,)), ((), ())),
+                    preferred_element_type=f32,
                 )
                 total = piece if total is None else total + piece
             result.append(total)
         return result
+
+    def apply_h(v):
+        return finish(mix(v))
 
     def inner(x, y):
         return partial([a * b for a, b in zip(x, y)])
@@ -245,9 +255,14 @@
         for q in range(nj):
             src[q] = value[q].astype(src.dtype)
         for k in range(T * R):
-            out_copy((k + 1) % (T * R), src, dst, which).start()
-
-    s0 = apply_h(v0)
+            out_copy((k + T * R // 2) % (T * R), src, dst, which).start()
+
+    mixed0 = mix(v0)
+    whole(pbuf, psem)
+    ip = [1.0 / pbuf[q].astype(f32) for q in range(nj)]
+    whole(rbuf.at[:, :, pl.ds(0, 3 * B // 4)], rsem)
+    complete(rbuf)
+    s0 = finish(mixed0)
     n_loc = lanes(inner(v0, v0))
     a_loc = lanes(inner(v0, s0))
     th_loc = a_loc / jnp.maximum(n_loc, 1e-30)

time: 33 us -> 32.9 us (level)
  no operation moved by 1% of the time
where the time goes in v5:
time: 32.9 us; the launch traced here: 32.8 us
  Pallas kernels  30.4 us (92%)
  between operations  2.41 us (7%)
    pallas_call x1, Pallas kernels, local(): pl.pallas_call(functools.partial(kernel, S, T, R, nj, count), out_shape=(...  28.3 us
    pallas_call x1, Pallas kernels, local(): pl.pallas_call(widen, out_shape=(wide, wide), in_specs=[hbm, hbm], out_sp...  2.02 us

profile of v5, /device:TPU:1, one launch (start us, length us, event | category | flops | bytes accessed | tf_op | source)
XLA Modules:
  0.0 32.8 jit_solution(16047810729436712515)
XLA Ops:
  0.6 28.3 %davidson.1 = (f32[1,4,256,128]{3,2,1,0:T(8,128)}, bf16[1,4,256,128]{3,2,1,0:T(8,128)(2,1)}, f32[1]{0:T(128)}) custom-call(bf16[1,4,256,128]{3,2,1,0:T(8,128)(2,1)} %v_in.1, bf16[1,4,256,128]{3,2,1,0:T(8,128)(2,1)} %p_in.1, bf16[1,1,4,256,256]{4,3,2,1,0:T(8,128)(2,1)} %l_in.1, bf16[1,1,4,256,128]{4,3,2,1,0:T(8,128)(2,1)} %r_in.1, s32[1,1,4]{2,1,0:T(1,128)} %used.1), custom_call_target="tpu_custom_call" | custom-call | tf_op jit(solution)/shard_map/davidson/pallas_call | solution.py:394
  29.0 2.0 %widen.1 = (f32[1,4,256,128]{3,2,1,0:T(8,128)}, f32[1,4,256,128]{3,2,1,0:T(8,128)}) custom-call(f32[1,4,256,128]{3,2,1,0:T(8,128)} %get-tuple-element.8.a_in, bf16[1,4,256,128]{3,2,1,0:T(8,128)(2,1)} %get-tuple-element.9.b_in), custom_call_target="tpu_custom_call" | custom-call | tf_op jit(solution)/shard_map/widen/pallas_call | solution.py:421
